TPU v7x, 128 devices: a whole 4x4x4 slice. The times are simulated.
128 devices in a mesh: kx: 16 (over z, x_lo, core), ky: 8 (over y, x_hi).
Axes of the slice: x: 4 (x_hi: 2, x_lo: 2; x = x_hi * 2 + x_lo), y: 4, z: 4, core: 2. Of those that a mesh axis runs over, the one named last changes fastest.
Arguments:
- crossed: bfloat16 [2, 80, 80, 6400], P(None, 'kx', 'ky'), may hold values from -6 to 6
- vertex: bfloat16 [80, 80, 6400], P('kx', 'ky'), may hold values from -0.625 to 0.625
- bubble: bfloat16 [80, 80, 16, 5, 5], P('kx', 'ky'), may hold values from -3 to 3
- pair_map: int32 [2, 25], replicated, may hold values from 0 to 24, each once within a row
- bond_shift: int32 [2, 5, 5, 2], replicated, may hold values from -2 to 2
- envelope: float32 [2, 80, 80], replicated, may hold values from 0.25 to 4
Outputs:
- correction: bfloat16 [80, 80, 6400], P('kx', 'ky')
Inputs may be any that keep to these rules, and one draw needn't show every extreme that they name: `pair_map`: each row names every form-factor pair once.
All inputs are finite; a program needn't handle non-finite values.
Results may differ from a plain program's by a relative error of at most 0.0095.
Values may be sent and summed in bfloat16 or wider, within the bound.
A program may use at most 64 MiB of HBM per device.

v0:
```python
import math

import jax
import jax.numpy as jnp
import ml_dtypes
import numpy as np
from jax import lax
from jax.experimental import pallas as pl
from jax.experimental.pallas import tpu as pltpu
from jax.sharding import PartitionSpec as P

LAT = 80
NFF = 5
NFREQ = 16
ORDER = 80
NX = 16
NY = 8
DEVICES = NX * NY
QX = LAT // NX
QY = LAT // NY
REACH = 2
SEND_ROWS = 40
BACK_ROWS = 24
UNROLL = 5
BF16 = ml_dtypes.bfloat16
MESH = pl.DeviceIdType.MESH


def cas_table(count):
    phases = np.outer(np.arange(count), np.arange(count)) % count
    angles = phases * (2.0 * math.pi / count)
    return ((np.cos(angles) + np.sin(angles)) / math.sqrt(count)).astype(np.float32)


CAS = cas_table(LAT)


def rolled_rows():
    rows = (np.arange(LAT)[None, :] + np.arange(-REACH, REACH + 1)[:, None]) % LAT
    return CAS[rows].astype(BF16)


def y_forward():
    reach = np.zeros((LAT, 128), np.float32)
    columns = np.arange(LAT + 2 * REACH)
    reach[:, columns] = CAS[:, (columns - REACH) % LAT]
    reach = reach.reshape(NY, QY, 128)
    table = np.zeros((NY, 2, QY, 2, 2, 2, 128), np.float32)
    for chan in range(2):
        for half in range(2):
            table[:, half, :, chan, chan, half] = reach
    return table.reshape(NY * SEND_ROWS, 4 * 128).astype(BF16)


def x_back():
    table = np.zeros((NX, 8, LAT), np.float32)
    table[:, :QX] = CAS.reshape(NX, QX, LAT)
    return table.reshape(NX * 8, LAT).astype(BF16)


def y_back():
    table = np.zeros((NY, 2, 12, 2, 128), np.float32)
    for half in range(2):
        table[:, half, :QY, half, :LAT] = CAS.reshape(NY, QY, LAT)
    return table.reshape(NY * BACK_ROWS, 2 * 128).astype(BF16)


def spread_source():
    table = np.zeros((112 + 400 + 112, 16 * 32), np.float32)
    a, n2, b = np.meshgrid(np.arange(5), np.arange(16), np.arange(5), indexing="ij")
    table[112 + 80 * a + 5 * n2 + b, 32 * n2 + 5 * a + b] = 1
    return table.astype(BF16)


def merge_x():
    table = np.zeros((5, 4, 32, 4, 128), np.float32)
    qx, g, pair = np.meshgrid(np.arange(5), np.arange(4), np.arange(25), indexing="ij")
    table[qx, g, pair, g, 25 * qx + pair] = 1
    return table.reshape(640, 512).astype(BF16)


def split_x():
    return np.ascontiguousarray(merge_x().T)


def gather_rows():
    table = np.zeros((16, 32, 5, 128), np.float32)
    a, n2, b = np.meshgrid(np.arange(5), np.arange(16), np.arange(5), indexing="ij")
    table[n2, 5 * a + b, a, 5 * n2 + b] = 1
    return table.reshape(512, 640).astype(BF16)


def turn_columns():
    table = np.zeros((80, 128), np.float32)
    n, a = np.meshgrid(np.arange(16), np.arange(5), indexing="ij")
    table[5 * n + a, 16 * a + n] = 1
    return table.astype(BF16)


def same_frequency():
    table = np.zeros((16, 128), np.float32)
    n, b = np.meshgrid(np.arange(16), np.arange(5), indexing="ij")
    table[n, 16 * b + n] = 1
    return table


def f32dot(left, right, dims=((1,), (0,))):
    return lax.dot_general(left, right, (dims, ((), ())), preferred_element_type=jnp.float32)


def build_slabs(crossed_ref, spread_ref, merge_ref, mixed_ref, slabs_ref):
    for n in range(NFREQ):
        start = 400 * n // 128 * 128
        offset = 400 * n - start
        spread = f32dot(crossed_ref[:, start : start + 512], spread_ref[112 - offset : 624 - offset, :])
        for part in range(4):
            for qx in range(QX):
                mixed_ref[part, qx, 20 * n : 20 * n + 20, :] = spread[
                    20 * qx : 20 * qx + 20, 128 * part : 128 * part + 128
                ]

    def one_part(part, carry):
        rows = jnp.concatenate([mixed_ref[part, qx] for qx in range(QX)], axis=1).astype(jnp.bfloat16)
        merged = f32dot(rows, merge_ref[...]).astype(jnp.bfloat16)
        for g in range(4):
            for pair in range(8):
                slabs_ref[(4 * part + g) * 8 + pair] = merged[
                    40 * pair : 40 * pair + 40, 128 * g : 128 * g + 128
                ]
        return carry

    lax.fori_loop(0, 4, one_part, 0)


def prepare_vertex(vertex_ref, bubble_ref, turn_ref, same_ref, rows_ref, left_ref, right_ref):
    for qx in range(QX):
        for i in range(ORDER):
            rows_ref[80 * i + 16 * qx : 80 * i + 16 * qx + 10, :80] = vertex_ref[
                qx, :, 80 * i : 80 * i + 80
            ].astype(jnp.float32)
    same = same_ref[...]

    def one(q, carry):
        at = q + 6 * (q // 10)
        block = jnp.concatenate(
            [rows_ref[pl.ds(80 * a + at, 16, stride=400), :] for a in range(5)], axis=0
        ).astype(jnp.bfloat16)
        bubble = jnp.concatenate(
            [bubble_ref[pl.ds(5 * q + a, 1), :] * same for a in range(5)], axis=0
        ).astype(jnp.bfloat16)
        turned = f32dot(block[:, :80], turn_ref[...]).astype(jnp.bfloat16)
        right_ref[q] = f32dot(turned[:, :80], bubble).astype(jnp.bfloat16)
        left = f32dot(bubble[:, :80], block)
        for a in range(5):
            left_ref[pl.ds(80 * q + a, 16, stride=5), :] = left[16 * a : 16 * a + 16]
        return carry

    lax.fori_loop(0, QX * QY, one, 0, unroll=5)


def finish(got_ref, split_ref, gather_ref, spread_ref, blocks_ref, left_ref, right_ref, rows_ref, out_ref):
    for part in range(4):
        rows = jnp.concatenate(
            [got_ref[8 * (4 * part + g) : 8 * (4 * part + g) + 8].reshape(192, 128) for g in range(4)], axis=1
        )
        apart = f32dot(rows, split_ref[...]).astype(jnp.bfloat16)
        for qx in range(QX):
            spread_ref[qx, :, 128 * part : 128 * part + 128] = apart[:, 128 * qx : 128 * qx + 128]
    for qx in range(QX):
        found = f32dot(spread_ref[qx], gather_ref[...])
        for a in range(5):
            blocks_ref[a, 192 * qx : 192 * qx + 192, :] = found[:, 128 * a : 128 * a + 128]

    def one(q, carry):
        at = q + 182 * (q // 10)
        block = jnp.concatenate(
            [blocks_ref[a, pl.ds(at, 16, stride=12), :] for a in range(5)], axis=0
        ).astype(jnp.bfloat16)
        left = left_ref[pl.ds(pl.multiple_of(80 * q, 8), 80), :].astype(jnp.bfloat16)
        result = f32dot(block[:, :80], left) + f32dot(right_ref[q][:, :80], block)
        put = q + 6 * (q // 10)
        for a in range(5):
            rows_ref[pl.ds(80 * a + put, 16, stride=400), :] = result[16 * a : 16 * a + 16]
        return carry

    lax.fori_loop(0, QX * QY, one, 0, unroll=5)
    for qx in range(QX):
        for i in range(0, ORDER, 8):
            wide = jnp.concatenate(
                [rows_ref[80 * (i + k) + 16 * qx : 80 * (i + k) + 16 * qx + 16, :80] for k in range(8)], axis=1
            ).astype(jnp.bfloat16)
            out_ref[qx, :, 80 * i : 80 * i + 640] = wide[:10]


def main_kernel(
    pair_ref, shift_ref, crossed_ref, vertex_ref, bubble_ref, envelope_ref,
    cas_ref, yf_ref, xb_ref, yb_ref, spread_ref, merge_ref, split_ref, gather_ref, turn_ref, same_ref,
    out_ref,
    mixed_ref, slabs_ref, recv_ref, half_ref, back_ref, outgoing_ref, got_ref,
    vertex_rows_ref, left_ref, right_ref, spread_back_ref, blocks_ref, out_rows_ref,
    send_sem, recv_sems, back_send_sem, back_sem,
):
    mx = lax.axis_index("kx")
    my = lax.axis_index("ky")
    me = mx * NY + my
    barrier = pltpu.get_barrier_semaphore()

    def partner(step):
        other = lax.rem(me + lax.rem(step * 37, DEVICES), DEVICES)
        return other, (other // NY, lax.rem(other, NY))

    def greet(step, carry):
        _, where = partner(step)
        pl.semaphore_signal(barrier, inc=1, device_id=where, device_id_type=MESH)
        return carry

    lax.fori_loop(1, DEVICES, greet, 0)
    build_slabs(crossed_ref, spread_ref, merge_ref, mixed_ref, slabs_ref)
    own = pltpu.make_async_copy(slabs_ref.at[me], recv_ref.at[me], recv_sems.at[mx])
    own.start()
    pl.semaphore_wait(barrier, DEVICES - 1)

    def send(step, carry):
        other, where = partner(step)
        pltpu.make_async_remote_copy(
            src_ref=slabs_ref.at[other],
            dst_ref=recv_ref.at[me],
            send_sem=send_sem,
            recv_sem=recv_sems.at[mx],
            device_id=where,
            device_id_type=MESH,
        ).start()
        return carry

    lax.fori_loop(1, DEVICES, send, 0)
    prepare_vertex(vertex_ref, bubble_ref, turn_ref, same_ref, vertex_rows_ref, left_ref, right_ref)

    for group in range(NX):
        here = pl.ds(NY * group, NY)
        pltpu.make_async_copy(slabs_ref.at[here], recv_ref.at[here], recv_sems.at[group]).wait()
        block = recv_ref[here].reshape(NY * SEND_ROWS, 128)
        turned = f32dot(block, yf_ref[...], ((0,), (0,)))
        for part in range(4):
            half_ref[part, 125 * group : 125 * group + 125, :] = turned[:125, 128 * part : 128 * part + 128]

    def one_pair(pair, carry):
        total = [None, None]
        for chan in range(2):
            source = pair_ref[chan, pair]
            step_x = shift_ref[chan, 2 * pair]
            step_y = shift_ref[chan, 2 * pair + 1]
            rows = pl.ds(source, LAT, stride=25)
            operand = jnp.concatenate(
                [half_ref[2 * chan + half, rows, :] for half in range(2)], axis=1
            ).astype(jnp.bfloat16)
            real = f32dot(cas_ref[step_x + REACH], operand)
            weight = envelope_ref[chan]
            for half in range(2):
                piece = pltpu.roll(real[:, 128 * half : 128 * half + 128], 128 - REACH - step_y, 1)
                term = piece * weight
                total[half] = term if chan == 0 else total[half] + term
        projected = jnp.concatenate(total, axis=1).astype(jnp.bfloat16)
        back = f32dot(xb_ref[...], projected)
        for half in range(2):
            back_ref[half, pl.ds(pair, 128, stride=25), :] = back[:, 128 * half : 128 * half + 128]
        return carry

    lax.fori_loop(0, 25, one_pair, 0, unroll=UNROLL)

    def one_group(step, carry):
        group = lax.rem(mx + step, NX)
        rows = pl.ds(pl.multiple_of(200 * group, 8), 128)
        operand = jnp.concatenate(
            [back_ref[half, rows, :] for half in range(2)], axis=1
        ).astype(jnp.bfloat16)
        result = f32dot(yb_ref[...], operand, ((1,), (1,))).astype(jnp.bfloat16)
        for lane in range(NY):
            outgoing_ref[NY * group + lane] = result[BACK_ROWS * lane : BACK_ROWS * lane + BACK_ROWS]

        def push(turn, inner):
            lane = lax.rem(my + turn, NY)
            other = NY * group + lane

            @pl.when(other != me)
            def _():
                pltpu.make_async_remote_copy(
                    src_ref=outgoing_ref.at[other],
                    dst_ref=got_ref.at[me],
                    send_sem=back_send_sem,
                    recv_sem=back_sem,
                    device_id=(group, lane),
                    device_id_type=MESH,
                ).start()

            @pl.when(other == me)
            def _():
                pltpu.make_async_copy(outgoing_ref.at[me], got_ref.at[me], back_sem).start()

            return inner

        lax.fori_loop(0, NY, push, 0)
        return carry

    lax.fori_loop(0, NX, one_group, 0)

    most = pl.ds(0, DEVICES - 1)
    pltpu.make_async_copy(slabs_ref.at[most], recv_ref.at[most], send_sem).wait()
    pltpu.make_async_copy(outgoing_ref, got_ref, back_sem).wait()
    finish(
        got_ref, split_ref, gather_ref, spread_back_ref, blocks_ref, left_ref, right_ref, out_rows_ref, out_ref
    )
    pltpu.make_async_copy(outgoing_ref.at[most], got_ref.at[most], back_send_sem).wait()


def local(crossed, vertex, bubble, pair_map, bond_shift, envelope):
    f32 = jnp.float32
    bf16 = jnp.bfloat16
    crossed = crossed.transpose(1, 2, 0, 3).reshape(QX * QY * 2, ORDER * ORDER)
    bubble = bubble.transpose(0, 1, 3, 4, 2).reshape(250, 80).astype(f32)
    bubble = jnp.pad(bubble, ((0, 0), (0, 48)))
    envelope = jnp.pad(envelope, ((0, 0), (0, 0), (0, 128 - LAT)))
    tables = [
        rolled_rows(), y_forward(), x_back(), y_back(), spread_source(), merge_x(), split_x(), gather_rows(),
        turn_columns(), same_frequency(),
    ]
    smem = pl.BlockSpec(memory_space=pltpu.SMEM)
    vmem = pl.BlockSpec(memory_space=pltpu.VMEM)
    return pl.pallas_call(
        main_kernel,
        out_shape=jax.ShapeDtypeStruct(vertex.shape, bf16),
        in_specs=[smem, smem] + [vmem] * (4 + len(tables)),
        out_specs=vmem,
        scratch_shapes=[
            pltpu.VMEM((4, QX, 20 * NFREQ, 128), f32),
            pltpu.VMEM((DEVICES, SEND_ROWS, 128), bf16),
            pltpu.VMEM((DEVICES, SEND_ROWS, 128), bf16),
            pltpu.VMEM((4, 25 * LAT, 128), f32),
            pltpu.VMEM((2, 25 * NX * 8, 128), f32),
            pltpu.VMEM((DEVICES, BACK_ROWS, 128), bf16),
            pltpu.VMEM((DEVICES, BACK_ROWS, 128), bf16),
            pltpu.VMEM((80 * ORDER, 128), f32),
            pltpu.VMEM((QX * QY * ORDER, 128), f32),
            pltpu.VMEM((QX * QY, ORDER, 128), bf16),
            pltpu.VMEM((QX, 192, 512), bf16),
            pltpu.VMEM((5, 192 * QX, 128), f32),
            pltpu.VMEM((80 * ORDER, 128), f32),
            pltpu.SemaphoreType.DMA,
            pltpu.SemaphoreType.DMA((NX,)),
            pltpu.SemaphoreType.DMA,
            pltpu.SemaphoreType.DMA,
        ],
        compiler_params=pltpu.CompilerParams(
            collective_id=0, has_side_effects=True, vmem_limit_bytes=56 * 2**20
        ),
    )(
        pair_map, bond_shift.reshape(2, 50), crossed, vertex, bubble, envelope,
        *[jnp.asarray(table) for table in tables],
    )


def solution(mesh):
    placed = (
        P(None, "kx", "ky", None),
        P("kx", "ky", None),
        P("kx", "ky", None, None, None),
        P(),
        P(),
        P(),
    )
    return jax.shard_map(
        local, mesh=mesh, in_specs=placed, out_specs=P("kx", "ky", None), check_vma=False
    )
```

profile of v0, /device:TPU:1, one launch (start us, length us, event | category | flops | bytes accessed | tf_op | source)
XLA Modules:
  0.0 71.4 jit_solution(13117852319923878618)
XLA Ops:
  0.0 0.8 %copy.18 = s32[2,5,5,2]{3,2,1,0:T(8,128)S(1)} copy(s32[2,5,5,2]{2,3,1,0:T(2,128)} %param.20) | data formatting | bytes 800 | tf_op args[4]
  0.8 0.7 reshape.9.shift_ref
  1.5 1.3 %convert_element_type.12 = bf16[250,80]{1,0:T(8,128)(2,1)S(1)} reshape(bf16[5,10,5,5,16]{4,3,2,1,0:T(8,128)(2,1)} %bitcast.3) | data formatting | bytes 80000 | tf_op jit(solution)/shard_map/convert_element_type | solution.py:319
  2.8 0.7 pad_convert_fusion.bubble_ref
  3.5 1.5 %pad.12.envelope_ref = f32[2,80,128]{2,1,0:T(8,128)} pad(f32[2,80,80]{2,1,0:T(8,128)} %param.21, f32[]{:T(128)} %constant.24.clone.1), padding=0_0x0_0x0_48 | pad | bytes 133124 | tf_op jit(solution)/shard_map/jit(_pad)/pad | solution.py:321
  5.0 3.8 %reshape.10.crossed_ref = bf16[100,6400]{1,0:T(8,128)(2,1)} reshape(bf16[5,10,2,6400]{3,2,1,0:T(2,128)(2,1)} %bitcast.2) | data formatting | bytes 2560000 | tf_op jit(solution)/shard_map/reshape | solution.py:318
  8.8 60.3 %shard_map.154 = bf16[5,10,6400]{2,1,0:T(8,128)(2,1)} custom-call(s32[2,25]{1,0:T(2,128)} %pair_ref.1, s32[2,50]{1,0:T(2,128)} %reshape.9.shift_ref, bf16[100,6400]{1,0:T(8,128)(2,1)} %reshape.10.crossed_ref, bf16[5,10,6400]{2,1,0:T(8,128)(2,1)} %vertex_ref.1, f32[250,128]{1,0:T(8,128)} %pad_convert_fusion.bubble_ref, f32[2,80,128]{2,1,0:T(8,128)} %pad.12.envelope_ref, ...), custom_call_target="tpu_custom_call" | custom-call | tf_op jit(solution)/shard_map/pallas_call | solution.py:328
  69.1 2.2 %copy.20 = bf16[5,10,6400]{2,1,0:T(8,128)(2,1)} copy(bf16[5,10,6400]{2,1,0:T(8,128)(2,1)} %shard_map.154) | data formatting | bytes 1280000
where the time goes:
time: 71.7 us; the launch traced here: 71.4 us
  Pallas kernels  60.3 us (84%)
  local copies, waits for them, and re-layouts  10.4 us (15%)
    pallas_call x1, Pallas kernels, local(): pl.pallas_call(main_kernel, out_shape=jax.ShapeDtypeStruct(vertex.shape,...  60.3 us
    reshape x1, local copies, waits for them, and re-layouts, local(): crossed = crossed.transpose(1, 2, 0, 3).reshape(QX * QY * 2, ORDER * ORDER)  3.8 us
    unnamed x2, local copies, waits for them, and re-layouts  3.08 us
    pad x1, local copies, waits for them, and re-layouts, local(): envelope = jnp.pad(envelope, ((0, 0), (0, 0), (0, 128 - LAT)))  1.53 us

commit v1 on v0

--- a/solution.py
+++ b/solution.py
@@ -112,7 +112,8 @@
     for n in range(NFREQ):
         start = 400 * n // 128 * 128
         offset = 400 * n - start
-        spread = f32dot(crossed_ref[:, start : start + 512], spread_ref[112 - offset : 624 - offset, :])
+        rows = crossed_ref[:, :, start : start + 512].reshape(2 * QX * QY, 512)
+        spread = f32dot(rows, spread_ref[112 - offset : 624 - offset, :])
         for part in range(4):
             for qx in range(QX):
                 mixed_ref[part, qx, 20 * n : 20 * n + 20, :] = spread[
@@ -132,13 +133,17 @@
     lax.fori_loop(0, 4, one_part, 0)
 
 
-def prepare_vertex(vertex_ref, bubble_ref, turn_ref, same_ref, rows_ref, left_ref, right_ref):
+def prepare_vertex(
+    vertex_ref, bubble_ref, turn_ref, same_ref, rows_ref, wide_ref, lines_ref, left_ref, right_ref
+):
     for qx in range(QX):
         for i in range(ORDER):
             rows_ref[80 * i + 16 * qx : 80 * i + 16 * qx + 10, :80] = vertex_ref[
                 qx, :, 80 * i : 80 * i + 80
             ].astype(jnp.float32)
     same = same_ref[...]
+    wide_ref[:, :5, :16] = bubble_ref[...].reshape(250, 5, 16).astype(jnp.float32)
+    lines_ref[:, :80] = jnp.concatenate([wide_ref[:, b, :16] for b in range(5)], axis=1)
 
     def one(q, carry):
         at = q + 6 * (q // 10)
@@ -146,7 +151,7 @@
             [rows_ref[pl.ds(80 * a + at, 16, stride=400), :] for a in range(5)], axis=0
         ).astype(jnp.bfloat16)
         bubble = jnp.concatenate(
-            [bubble_ref[pl.ds(5 * q + a, 1), :] * same for a in range(5)], axis=0
+            [lines_ref[pl.ds(5 * q + a, 1), :] * same for a in range(5)], axis=0
         ).astype(jnp.bfloat16)
         turned = f32dot(block[:, :80], turn_ref[...]).astype(jnp.bfloat16)
         right_ref[q] = f32dot(turned[:, :80], bubble).astype(jnp.bfloat16)
@@ -193,13 +198,22 @@
 
 
 def main_kernel(
-    pair_ref, shift_ref, crossed_ref, vertex_ref, bubble_ref, envelope_ref,
-    cas_ref, yf_ref, xb_ref, yb_ref, spread_ref, merge_ref, split_ref, gather_ref, turn_ref, same_ref,
+    pair_ref, shift_ref, envelope_ref, xb_ref, yb_ref, turn_ref, same_ref,
+    crossed_hbm, spread_hbm, merge_hbm, vertex_hbm, bubble_hbm, yf_hbm, cas_hbm, split_hbm, gather_hbm,
     out_ref,
-    mixed_ref, slabs_ref, recv_ref, half_ref, back_ref, outgoing_ref, got_ref,
-    vertex_rows_ref, left_ref, right_ref, spread_back_ref, blocks_ref, out_rows_ref,
-    send_sem, recv_sems, back_send_sem, back_sem,
+    crossed_ref, spread_ref, merge_ref, vertex_ref, bubble_ref, yf_ref, cas_ref, split_ref, gather_ref,
+    mixed_ref, slabs_ref, recv_ref, half_ref, back_ref, outgoing_ref, got_ref, weight_ref,
+    vertex_rows_ref, wide_ref, lines_ref, left_ref, right_ref, spread_back_ref, blocks_ref, out_rows_ref,
+    load_sems, send_sem, recv_sems, back_send_sem, back_sem,
 ):
+    sources = (crossed_hbm, spread_hbm, merge_hbm, vertex_hbm, bubble_hbm, yf_hbm, cas_hbm, split_hbm, gather_hbm)
+    places = (crossed_ref, spread_ref, merge_ref, vertex_ref, bubble_ref, yf_ref, cas_ref, split_ref, gather_ref)
+    loads = [
+        pltpu.make_async_copy(source, place, load_sems.at[k])
+        for k, (source, place) in enumerate(zip(sources, places))
+    ]
+    for load in loads:
+        load.start()
     mx = lax.axis_index("kx")
     my = lax.axis_index("ky")
     me = mx * NY + my
@@ -215,6 +229,8 @@
         return carry
 
     lax.fori_loop(1, DEVICES, greet, 0)
+    for load in loads[:3]:
+        load.wait()
     build_slabs(crossed_ref, spread_ref, merge_ref, mixed_ref, slabs_ref)
     own = pltpu.make_async_copy(slabs_ref.at[me], recv_ref.at[me], recv_sems.at[mx])
     own.start()
@@ -233,7 +249,13 @@
         return carry
 
     lax.fori_loop(1, DEVICES, send, 0)
-    prepare_vertex(vertex_ref, bubble_ref, turn_ref, same_ref, vertex_rows_ref, left_ref, right_ref)
+    weight_ref[...] = jnp.zeros_like(weight_ref)
+    weight_ref[:, :, :LAT] = envelope_ref[...]
+    for load in loads[3:]:
+        load.wait()
+    prepare_vertex(
+        vertex_ref, bubble_ref, turn_ref, same_ref, vertex_rows_ref, wide_ref, lines_ref, left_ref, right_ref
+    )
 
     for group in range(NX):
         here = pl.ds(NY * group, NY)
@@ -247,14 +269,14 @@
         total = [None, None]
         for chan in range(2):
             source = pair_ref[chan, pair]
-            step_x = shift_ref[chan, 2 * pair]
-            step_y = shift_ref[chan, 2 * pair + 1]
+            step_x = shift_ref[chan, pair // 5, 0, lax.rem(pair, 5)]
+            step_y = shift_ref[chan, pair // 5, 1, lax.rem(pair, 5)]
             rows = pl.ds(source, LAT, stride=25)
             operand = jnp.concatenate(
                 [half_ref[2 * chan + half, rows, :] for half in range(2)], axis=1
             ).astype(jnp.bfloat16)
             real = f32dot(cas_ref[step_x + REACH], operand)
-            weight = envelope_ref[chan]
+            weight = weight_ref[chan]
             for half in range(2):
                 piece = pltpu.roll(real[:, 128 * half : 128 * half + 128], 128 - REACH - step_y, 1)
                 term = piece * weight
@@ -315,22 +337,24 @@
 def local(crossed, vertex, bubble, pair_map, bond_shift, envelope):
     f32 = jnp.float32
     bf16 = jnp.bfloat16
-    crossed = crossed.transpose(1, 2, 0, 3).reshape(QX * QY * 2, ORDER * ORDER)
-    bubble = bubble.transpose(0, 1, 3, 4, 2).reshape(250, 80).astype(f32)
-    bubble = jnp.pad(bubble, ((0, 0), (0, 48)))
-    envelope = jnp.pad(envelope, ((0, 0), (0, 0), (0, 128 - LAT)))
-    tables = [
-        rolled_rows(), y_forward(), x_back(), y_back(), spread_source(), merge_x(), split_x(), gather_rows(),
-        turn_columns(), same_frequency(),
+    crossed = crossed.transpose(1, 2, 0, 3).reshape(QX * QY, 2, ORDER * ORDER)
+    bubble = bubble.transpose(0, 1, 3, 4, 2).reshape(QX * QY, NFF, NFF, NFREQ)
+    bond_shift = bond_shift.transpose(0, 1, 3, 2)
+    small = [x_back(), y_back(), turn_columns(), same_frequency()]
+    small = [jnp.asarray(table) for table in small]
+    large = [
+        crossed, jnp.asarray(spread_source()), jnp.asarray(merge_x()), vertex, bubble,
+        jnp.asarray(y_forward()), jnp.asarray(rolled_rows()), jnp.asarray(split_x()), jnp.asarray(gather_rows()),
     ]
     smem = pl.BlockSpec(memory_space=pltpu.SMEM)
     vmem = pl.BlockSpec(memory_space=pltpu.VMEM)
+    hbm = pl.BlockSpec(memory_space=pl.ANY)
     return pl.pallas_call(
         main_kernel,
         out_shape=jax.ShapeDtypeStruct(vertex.shape, bf16),
-        in_specs=[smem, smem] + [vmem] * (4 + len(tables)),
+        in_specs=[smem, smem, vmem] + [vmem] * len(small) + [hbm] * len(large),
         out_specs=vmem,
-        scratch_shapes=[
+        scratch_shapes=[pltpu.VMEM(array.shape, array.dtype) for array in large] + [
             pltpu.VMEM((4, QX, 20 * NFREQ, 128), f32),
             pltpu.VMEM((DEVICES, SEND_ROWS, 128), bf16),
             pltpu.VMEM((DEVICES, SEND_ROWS, 128), bf16),
@@ -338,24 +362,25 @@
             pltpu.VMEM((2, 25 * NX * 8, 128), f32),
             pltpu.VMEM((DEVICES, BACK_ROWS, 128), bf16),
             pltpu.VMEM((DEVICES, BACK_ROWS, 128), bf16),
+            pltpu.VMEM((2, LAT, 128), f32),
             pltpu.VMEM((80 * ORDER, 128), f32),
+            pltpu.VMEM((250, 8, 128), f32),
+            pltpu.VMEM((250, 128), f32),
             pltpu.VMEM((QX * QY * ORDER, 128), f32),
             pltpu.VMEM((QX * QY, ORDER, 128), bf16),
             pltpu.VMEM((QX, 192, 512), bf16),
             pltpu.VMEM((5, 192 * QX, 128), f32),
             pltpu.VMEM((80 * ORDER, 128), f32),
+            pltpu.SemaphoreType.DMA((len(large),)),
             pltpu.SemaphoreType.DMA,
             pltpu.SemaphoreType.DMA((NX,)),
             pltpu.SemaphoreType.DMA,
             pltpu.SemaphoreType.DMA,
         ],
         compiler_params=pltpu.CompilerParams(
-            collective_id=0, has_side_effects=True, vmem_limit_bytes=56 * 2**20
+            collective_id=0, has_side_effects=True, vmem_limit_bytes=60 * 2**20
         ),
-    )(
-        pair_map, bond_shift.reshape(2, 50), crossed, vertex, bubble, envelope,
-        *[jnp.asarray(table) for table in tables],
-    )
+    )(pair_map, bond_shift, envelope, *small, *large)
 
 
 def solution(mesh):

time: 71.7 us -> 61.2 us (0.85)
  local copies, waits for them, and re-layouts: 10.4 us -> 2.24 us
  Pallas kernels: 60.3 us -> 58.7 us
    reshape x2 -> x0, local copies, waits for them, and re-layouts: 4.48 us -> none  [the longest x1 3.8 us: local(): crossed = crossed.transpose(1, 2, 0, 3).reshape(QX * QY * 2, ORDER * ORDER)]
    pallas_call x1, Pallas kernels: 60.3 us -> 58.7 us  [local(): pl.pallas_call(main_kernel, out_shape=jax.ShapeDtypeStruct(vertex.shape,...]
    pad x1 -> x0, local copies, waits for them, and re-layouts: 1.53 us -> none  [local(): envelope = jnp.pad(envelope, ((0, 0), (0, 0), (0, 128 - LAT)))]
    convert_element_type x1 -> x0, local copies, waits for them, and re-layouts: 1.32 us -> none  [local(): bubble = bubble.transpose(0, 1, 3, 4, 2).reshape(250, 80).astype(f32)]
    unnamed x2 -> x1, local copies, waits for them, and re-layouts: 3.08 us -> 2.24 us
where the time goes in v1:
time: 61.2 us; the launch traced here: 61 us
  Pallas kernels  58.7 us (96%)
  local copies, waits for them, and re-layouts  2.24 us (4%)
    pallas_call x1, Pallas kernels, local(): pl.pallas_call(main_kernel, out_shape=jax.ShapeDtypeStruct(vertex.shape,...  58.7 us
    unnamed x1, local copies, waits for them, and re-layouts  2.24 us

profile of v1, /device:TPU:1, one launch (start us, length us, event | category | flops | bytes accessed | tf_op | source)
XLA Modules:
  0.0 61.0 jit_solution(16387193357553880347)
XLA Ops:
  0.0 58.7 %shard_map.154 = bf16[5,10,6400]{2,1,0:T(8,128)(2,1)} custom-call(s32[2,25]{1,0:T(2,128)} %pair_ref.1, s32[2,5,2,5]{3,2,1,0:T(2,128)} %bitcast.9, f32[2,80,80]{2,1,0:T(8,128)} %envelope_ref.1, bf16[128,80]{1,0:T(8,128)(2,1)} %constant.20.clone.xb_ref, bf16[192,256]{1,0:T(8,128)(2,1)} %constant.21.clone.yb_ref, bf16[80,128]{1,0:T(8,128)(2,1)} %constant.22.clone.turn_ref, ...), custom_call_target="tpu_custom_call" | custom-call | tf_op jit(solution)/shard_map/pallas_call | solution.py:352
  58.7 2.2 %copy.18 = bf16[5,10,6400]{2,1,0:T(8,128)(2,1)} copy(bf16[5,10,6400]{2,1,0:T(8,128)(2,1)} %shard_map.154) | data formatting | bytes 1280000

commit v2 on v1

--- a/solution.py
+++ b/solution.py
@@ -21,7 +21,7 @@
 REACH = 2
 SEND_ROWS = 40
 BACK_ROWS = 24
-UNROLL = 5
+BATCH = 25
 BF16 = ml_dtypes.bfloat16
 MESH = pl.DeviceIdType.MESH
 
@@ -130,7 +130,8 @@
                 ]
         return carry
 
-    lax.fori_loop(0, 4, one_part, 0)
+    for part in range(4):
+        one_part(part, 0)
 
 
 def prepare_vertex(
@@ -145,50 +146,57 @@
     wide_ref[:, :5, :16] = bubble_ref[...].reshape(250, 5, 16).astype(jnp.float32)
     lines_ref[:, :80] = jnp.concatenate([wide_ref[:, b, :16] for b in range(5)], axis=1)
 
-    def one(q, carry):
-        at = q + 6 * (q // 10)
-        block = jnp.concatenate(
-            [rows_ref[pl.ds(80 * a + at, 16, stride=400), :] for a in range(5)], axis=0
-        ).astype(jnp.bfloat16)
-        bubble = jnp.concatenate(
-            [lines_ref[pl.ds(5 * q + a, 1), :] * same for a in range(5)], axis=0
-        ).astype(jnp.bfloat16)
-        turned = f32dot(block[:, :80], turn_ref[...]).astype(jnp.bfloat16)
-        right_ref[q] = f32dot(turned[:, :80], bubble).astype(jnp.bfloat16)
-        left = f32dot(bubble[:, :80], block)
-        for a in range(5):
-            left_ref[pl.ds(80 * q + a, 16, stride=5), :] = left[16 * a : 16 * a + 16]
-        return carry
-
-    lax.fori_loop(0, QX * QY, one, 0, unroll=5)
-
-
-def finish(got_ref, split_ref, gather_ref, spread_ref, blocks_ref, left_ref, right_ref, rows_ref, out_ref):
-    for part in range(4):
-        rows = jnp.concatenate(
-            [got_ref[8 * (4 * part + g) : 8 * (4 * part + g) + 8].reshape(192, 128) for g in range(4)], axis=1
-        )
-        apart = f32dot(rows, split_ref[...]).astype(jnp.bfloat16)
-        for qx in range(QX):
-            spread_ref[qx, :, 128 * part : 128 * part + 128] = apart[:, 128 * qx : 128 * qx + 128]
+    for start in range(0, QX * QY, BATCH):
+        batch = range(start, start + BATCH)
+        blocks = []
+        bubbles = []
+        for q in batch:
+            at = q + 6 * (q // 10)
+            blocks.append(
+                jnp.concatenate(
+                    [rows_ref[pl.ds(80 * a + at, 16, stride=400), :] for a in range(5)], axis=0
+                ).astype(jnp.bfloat16)
+            )
+            bubbles.append(
+                jnp.concatenate(
+                    [lines_ref[pl.ds(5 * q + a, 1), :] * same for a in range(5)], axis=0
+                ).astype(jnp.bfloat16)
+            )
+        turned = [f32dot(block[:, :80], turn_ref[...]).astype(jnp.bfloat16) for block in blocks]
+        for q, block, bubble in zip(batch, blocks, bubbles):
+            left = f32dot(bubble[:, :80], block)
+            for a in range(5):
+                left_ref[pl.ds(80 * q + a, 16, stride=5), :] = left[16 * a : 16 * a + 16]
+        for q, bubble, matrix in zip(batch, bubbles, turned):
+            right_ref[q] = f32dot(matrix[:, :80], bubble).astype(jnp.bfloat16)
+
+
+def finish_part(part, got_ref, split_ref, spread_ref):
+    rows = jnp.concatenate(
+        [got_ref[8 * (4 * part + g) : 8 * (4 * part + g) + 8].reshape(192, 128) for g in range(4)], axis=1
+    )
+    apart = f32dot(rows, split_ref[...]).astype(jnp.bfloat16)
+    for qx in range(QX):
+        spread_ref[qx, :, 128 * part : 128 * part + 128] = apart[:, 128 * qx : 128 * qx + 128]
+
+
+def finish(gather_ref, spread_ref, blocks_ref, left_ref, right_ref, rows_ref, out_ref):
     for qx in range(QX):
         found = f32dot(spread_ref[qx], gather_ref[...])
         for a in range(5):
             blocks_ref[a, 192 * qx : 192 * qx + 192, :] = found[:, 128 * a : 128 * a + 128]
 
-    def one(q, carry):
+    for q in range(QX * QY):
         at = q + 182 * (q // 10)
         block = jnp.concatenate(
             [blocks_ref[a, pl.ds(at, 16, stride=12), :] for a in range(5)], axis=0
         ).astype(jnp.bfloat16)
-        left = left_ref[pl.ds(pl.multiple_of(80 * q, 8), 80), :].astype(jnp.bfloat16)
+        left = left_ref[80 * q : 80 * q + 80, :].astype(jnp.bfloat16)
         result = f32dot(block[:, :80], left) + f32dot(right_ref[q][:, :80], block)
         put = q + 6 * (q // 10)
         for a in range(5):
             rows_ref[pl.ds(80 * a + put, 16, stride=400), :] = result[16 * a : 16 * a + 16]
-        return carry
-
-    lax.fori_loop(0, QX * QY, one, 0, unroll=5)
+
     for qx in range(QX):
         for i in range(0, ORDER, 8):
             wide = jnp.concatenate(
@@ -204,7 +212,7 @@
     crossed_ref, spread_ref, merge_ref, vertex_ref, bubble_ref, yf_ref, cas_ref, split_ref, gather_ref,
     mixed_ref, slabs_ref, recv_ref, half_ref, back_ref, outgoing_ref, got_ref, weight_ref,
     vertex_rows_ref, wide_ref, lines_ref, left_ref, right_ref, spread_back_ref, blocks_ref, out_rows_ref,
-    load_sems, send_sem, recv_sems, back_send_sem, back_sem,
+    load_sems, send_sem, recv_sems, back_send_sem, back_sems,
 ):
     sources = (crossed_hbm, spread_hbm, merge_hbm, vertex_hbm, bubble_hbm, yf_hbm, cas_hbm, split_hbm, gather_hbm)
     places = (crossed_ref, spread_ref, merge_ref, vertex_ref, bubble_ref, yf_ref, cas_ref, split_ref, gather_ref)
@@ -248,7 +256,7 @@
         ).start()
         return carry
 
-    lax.fori_loop(1, DEVICES, send, 0)
+    lax.fori_loop(1, DEVICES, send, 0, unroll=True)
     weight_ref[...] = jnp.zeros_like(weight_ref)
     weight_ref[:, :, :LAT] = envelope_ref[...]
     for load in loads[3:]:
@@ -265,31 +273,31 @@
         for part in range(4):
             half_ref[part, 125 * group : 125 * group + 125, :] = turned[:125, 128 * part : 128 * part + 128]
 
-    def one_pair(pair, carry):
-        total = [None, None]
+    reals = []
+    for pair in range(25):
         for chan in range(2):
-            source = pair_ref[chan, pair]
-            step_x = shift_ref[chan, pair // 5, 0, lax.rem(pair, 5)]
-            step_y = shift_ref[chan, pair // 5, 1, lax.rem(pair, 5)]
-            rows = pl.ds(source, LAT, stride=25)
+            rows = pl.ds(pair_ref[chan, pair], LAT, stride=25)
             operand = jnp.concatenate(
                 [half_ref[2 * chan + half, rows, :] for half in range(2)], axis=1
             ).astype(jnp.bfloat16)
-            real = f32dot(cas_ref[step_x + REACH], operand)
-            weight = weight_ref[chan]
+            step_x = shift_ref[chan, pair // 5, 0, pair % 5]
+            reals.append(f32dot(cas_ref[step_x + REACH], operand))
+    projected = []
+    for pair in range(25):
+        total = [None, None]
+        for chan in range(2):
+            step_y = shift_ref[chan, pair // 5, 1, pair % 5]
             for half in range(2):
-                piece = pltpu.roll(real[:, 128 * half : 128 * half + 128], 128 - REACH - step_y, 1)
-                term = piece * weight
+                piece = reals[2 * pair + chan][:, 128 * half : 128 * half + 128]
+                term = pltpu.roll(piece, 128 - REACH - step_y, 1) * weight_ref[chan]
                 total[half] = term if chan == 0 else total[half] + term
-        projected = jnp.concatenate(total, axis=1).astype(jnp.bfloat16)
-        back = f32dot(xb_ref[...], projected)
+        projected.append(jnp.concatenate(total, axis=1).astype(jnp.bfloat16))
+    for pair in range(25):
+        back = f32dot(xb_ref[...], projected[pair])
         for half in range(2):
             back_ref[half, pl.ds(pair, 128, stride=25), :] = back[:, 128 * half : 128 * half + 128]
-        return carry
-
-    lax.fori_loop(0, 25, one_pair, 0, unroll=UNROLL)
-
-    def one_group(step, carry):
+
+    for step in range(NX):
         group = lax.rem(mx + step, NX)
         rows = pl.ds(pl.multiple_of(200 * group, 8), 128)
         operand = jnp.concatenate(
@@ -298,39 +306,27 @@
         result = f32dot(yb_ref[...], operand, ((1,), (1,))).astype(jnp.bfloat16)
         for lane in range(NY):
             outgoing_ref[NY * group + lane] = result[BACK_ROWS * lane : BACK_ROWS * lane + BACK_ROWS]
-
-        def push(turn, inner):
+        for turn in range(NY):
             lane = lax.rem(my + turn, NY)
-            other = NY * group + lane
-
-            @pl.when(other != me)
-            def _():
+            if step == 0 and turn == 0:
+                pltpu.make_async_copy(outgoing_ref.at[me], got_ref.at[me], back_sems.at[mx // 4]).start()
+            else:
                 pltpu.make_async_remote_copy(
-                    src_ref=outgoing_ref.at[other],
+                    src_ref=outgoing_ref.at[NY * group + lane],
                     dst_ref=got_ref.at[me],
                     send_sem=back_send_sem,
-                    recv_sem=back_sem,
+                    recv_sem=back_sems.at[mx // 4],
                     device_id=(group, lane),
                     device_id_type=MESH,
                 ).start()
 
-            @pl.when(other == me)
-            def _():
-                pltpu.make_async_copy(outgoing_ref.at[me], got_ref.at[me], back_sem).start()
-
-            return inner
-
-        lax.fori_loop(0, NY, push, 0)
-        return carry
-
-    lax.fori_loop(0, NX, one_group, 0)
-
     most = pl.ds(0, DEVICES - 1)
     pltpu.make_async_copy(slabs_ref.at[most], recv_ref.at[most], send_sem).wait()
-    pltpu.make_async_copy(outgoing_ref, got_ref, back_sem).wait()
-    finish(
-        got_ref, split_ref, gather_ref, spread_back_ref, blocks_ref, left_ref, right_ref, out_rows_ref, out_ref
-    )
+    for part in range(4):
+        here = pl.ds(32 * part, 32)
+        pltpu.make_async_copy(outgoing_ref.at[here], got_ref.at[here], back_sems.at[part]).wait()
+        finish_part(part, got_ref, split_ref, spread_back_ref)
+    finish(gather_ref, spread_back_ref, blocks_ref, left_ref, right_ref, out_rows_ref, out_ref)
     pltpu.make_async_copy(outgoing_ref.at[most], got_ref.at[most], back_send_sem).wait()
 
 
@@ -375,7 +371,7 @@
             pltpu.SemaphoreType.DMA,
             pltpu.SemaphoreType.DMA((NX,)),
             pltpu.SemaphoreType.DMA,
-            pltpu.SemaphoreType.DMA,
+            pltpu.SemaphoreType.DMA((4,)),
         ],
         compiler_params=pltpu.CompilerParams(
             collective_id=0, has_side_effects=True, vmem_limit_bytes=60 * 2**20

time: 61.2 us -> 55.7 us (0.910)
  Pallas kernels: 58.7 us -> 53.3 us
    pallas_call x1, Pallas kernels: 58.7 us -> 53.3 us  [local(): pl.pallas_call(main_kernel, out_shape=jax.ShapeDtypeStruct(vertex.shape,...]
where the time goes in v2:
time: 55.7 us; the launch traced here: 55.6 us
  Pallas kernels  53.3 us (96%)
  local copies, waits for them, and re-layouts  2.24 us (4%)
    pallas_call x1, Pallas kernels, local(): pl.pallas_call(main_kernel, out_shape=jax.ShapeDtypeStruct(vertex.shape,...  53.3 us
    unnamed x1, local copies, waits for them, and re-layouts  2.24 us

profile of v2, /device:TPU:1, one launch (start us, length us, event | category | flops | bytes accessed | tf_op | source)
XLA Modules:
  0.0 55.6 jit_solution(14798001531003819439)
XLA Ops:
  0.0 53.3 %shard_map.154 = bf16[5,10,6400]{2,1,0:T(8,128)(2,1)} custom-call(s32[2,25]{1,0:T(2,128)} %pair_ref.1, s32[2,5,2,5]{3,2,1,0:T(2,128)} %bitcast.9, f32[2,80,80]{2,1,0:T(8,128)} %envelope_ref.1, bf16[128,80]{1,0:T(8,128)(2,1)} %constant.20.clone.xb_ref, bf16[192,256]{1,0:T(8,128)(2,1)} %constant.21.clone.yb_ref, bf16[80,128]{1,0:T(8,128)(2,1)} %constant.22.clone.turn_ref, ...), custom_call_target="tpu_custom_call" | custom-call | tf_op jit(solution)/shard_map/pallas_call | solution.py:348
  53.3 2.2 %copy.18 = bf16[5,10,6400]{2,1,0:T(8,128)(2,1)} copy(bf16[5,10,6400]{2,1,0:T(8,128)(2,1)} %shard_map.154) | data formatting | bytes 1280000

commit v3 on v2

--- a/solution.py
+++ b/solution.py
@@ -102,6 +102,24 @@
     n, b = np.meshgrid(np.arange(16), np.arange(5), indexing="ij")
     table[n, 16 * b + n] = 1
     return table
+
+
+def partner_order():
+    offsets = [(z, y, x, c) for z in range(4) for y in range(4) for x in range(4) for c in range(2)]
+    links = [sum(min(step, 4 - step) for step in offset[:3]) for offset in offsets]
+    ranked = sorted(zip(links, offsets), key=lambda pair: -pair[0])
+    return [offset for _, offset in ranked if offset != (0, 0, 0, 0)]
+
+
+def partners(mx, my):
+    mz, my_y = mx // 4, my // 2
+    mine_x = lax.rem(my, 2) * 2 + lax.rem(mx // 2, 2)
+    mine_core = lax.rem(mx, 2)
+    for z, y, x, core in partner_order():
+        there = lax.rem(mine_x + x, 4)
+        kx = lax.rem(mz + z, 4) * 4 + lax.rem(there, 2) * 2 + lax.rem(mine_core + core, 2)
+        ky = lax.rem(my_y + y, 4) * 2 + there // 2
+        yield kx, ky
 
 
 def f32dot(left, right, dims=((1,), (0,))):
@@ -205,21 +223,18 @@
             out_ref[qx, :, 80 * i : 80 * i + 640] = wide[:10]
 
 
-def main_kernel(
-    pair_ref, shift_ref, envelope_ref, xb_ref, yb_ref, turn_ref, same_ref,
-    crossed_hbm, spread_hbm, merge_hbm, vertex_hbm, bubble_hbm, yf_hbm, cas_hbm, split_hbm, gather_hbm,
-    out_ref,
-    crossed_ref, spread_ref, merge_ref, vertex_ref, bubble_ref, yf_ref, cas_ref, split_ref, gather_ref,
-    mixed_ref, slabs_ref, recv_ref, half_ref, back_ref, outgoing_ref, got_ref, weight_ref,
-    vertex_rows_ref, wide_ref, lines_ref, left_ref, right_ref, spread_back_ref, blocks_ref, out_rows_ref,
-    load_sems, send_sem, recv_sems, back_send_sem, back_sems,
-):
-    sources = (crossed_hbm, spread_hbm, merge_hbm, vertex_hbm, bubble_hbm, yf_hbm, cas_hbm, split_hbm, gather_hbm)
-    places = (crossed_ref, spread_ref, merge_ref, vertex_ref, bubble_ref, yf_ref, cas_ref, split_ref, gather_ref)
-    loads = [
-        pltpu.make_async_copy(source, place, load_sems.at[k])
-        for k, (source, place) in enumerate(zip(sources, places))
-    ]
+def main_kernel(*refs):
+    (
+        crossed_hbm, spread_hbm, merge_hbm, pair_hbm, shift_hbm, envelope_hbm, vertex_hbm, bubble_hbm, same_hbm,
+        turn_hbm, yf_hbm, cas_hbm, xb_hbm, yb_hbm, split_hbm, gather_hbm,
+        out_ref,
+        crossed_ref, spread_ref, merge_ref, pair_ref, shift_ref, envelope_ref, vertex_ref, bubble_ref, same_ref,
+        turn_ref, yf_ref, cas_ref, xb_ref, yb_ref, split_ref, gather_ref,
+        mixed_ref, slabs_ref, recv_ref, half_ref, back_ref, outgoing_ref, got_ref, weight_ref,
+        vertex_rows_ref, wide_ref, lines_ref, left_ref, right_ref, spread_back_ref, blocks_ref, out_rows_ref,
+        load_sems, send_sem, recv_sems, back_send_sem, back_sems,
+    ) = refs
+    loads = [pltpu.make_async_copy(refs[k], refs[17 + k], load_sems.at[k]) for k in range(16)]
     for load in loads:
         load.start()
     mx = lax.axis_index("kx")
@@ -227,16 +242,8 @@
     me = mx * NY + my
     barrier = pltpu.get_barrier_semaphore()
 
-    def partner(step):
-        other = lax.rem(me + lax.rem(step * 37, DEVICES), DEVICES)
-        return other, (other // NY, lax.rem(other, NY))
-
-    def greet(step, carry):
-        _, where = partner(step)
-        pl.semaphore_signal(barrier, inc=1, device_id=where, device_id_type=MESH)
-        return carry
-
-    lax.fori_loop(1, DEVICES, greet, 0)
+    for kx, ky in partners(mx, my):
+        pl.semaphore_signal(barrier, inc=1, device_id=(kx, ky), device_id_type=MESH)
     for load in loads[:3]:
         load.wait()
     build_slabs(crossed_ref, spread_ref, merge_ref, mixed_ref, slabs_ref)
@@ -244,23 +251,20 @@
     own.start()
     pl.semaphore_wait(barrier, DEVICES - 1)
 
-    def send(step, carry):
-        other, where = partner(step)
+    for kx, ky in partners(mx, my):
         pltpu.make_async_remote_copy(
-            src_ref=slabs_ref.at[other],
+            src_ref=slabs_ref.at[kx * NY + ky],
             dst_ref=recv_ref.at[me],
             send_sem=send_sem,
             recv_sem=recv_sems.at[mx],
-            device_id=where,
+            device_id=(kx, ky),
             device_id_type=MESH,
         ).start()
-        return carry
-
-    lax.fori_loop(1, DEVICES, send, 0, unroll=True)
+
+    for load in loads[3:]:
+        load.wait()
     weight_ref[...] = jnp.zeros_like(weight_ref)
     weight_ref[:, :, :LAT] = envelope_ref[...]
-    for load in loads[3:]:
-        load.wait()
     prepare_vertex(
         vertex_ref, bubble_ref, turn_ref, same_ref, vertex_rows_ref, wide_ref, lines_ref, left_ref, right_ref
     )
@@ -297,28 +301,24 @@
         for half in range(2):
             back_ref[half, pl.ds(pair, 128, stride=25), :] = back[:, 128 * half : 128 * half + 128]
 
-    for step in range(NX):
-        group = lax.rem(mx + step, NX)
-        rows = pl.ds(pl.multiple_of(200 * group, 8), 128)
+    for group in range(NX):
+        rows = pl.ds(200 * group, 128)
         operand = jnp.concatenate(
             [back_ref[half, rows, :] for half in range(2)], axis=1
         ).astype(jnp.bfloat16)
         result = f32dot(yb_ref[...], operand, ((1,), (1,))).astype(jnp.bfloat16)
         for lane in range(NY):
             outgoing_ref[NY * group + lane] = result[BACK_ROWS * lane : BACK_ROWS * lane + BACK_ROWS]
-        for turn in range(NY):
-            lane = lax.rem(my + turn, NY)
-            if step == 0 and turn == 0:
-                pltpu.make_async_copy(outgoing_ref.at[me], got_ref.at[me], back_sems.at[mx // 4]).start()
-            else:
-                pltpu.make_async_remote_copy(
-                    src_ref=outgoing_ref.at[NY * group + lane],
-                    dst_ref=got_ref.at[me],
-                    send_sem=back_send_sem,
-                    recv_sem=back_sems.at[mx // 4],
-                    device_id=(group, lane),
-                    device_id_type=MESH,
-                ).start()
+    pltpu.make_async_copy(outgoing_ref.at[me], got_ref.at[me], back_sems.at[mx // 4]).start()
+    for kx, ky in partners(mx, my):
+        pltpu.make_async_remote_copy(
+            src_ref=outgoing_ref.at[kx * NY + ky],
+            dst_ref=got_ref.at[me],
+            send_sem=back_send_sem,
+            recv_sem=back_sems.at[mx // 4],
+            device_id=(kx, ky),
+            device_id_type=MESH,
+        ).start()
 
     most = pl.ds(0, DEVICES - 1)
     pltpu.make_async_copy(slabs_ref.at[most], recv_ref.at[most], send_sem).wait()
@@ -336,21 +336,21 @@
     crossed = crossed.transpose(1, 2, 0, 3).reshape(QX * QY, 2, ORDER * ORDER)
     bubble = bubble.transpose(0, 1, 3, 4, 2).reshape(QX * QY, NFF, NFF, NFREQ)
     bond_shift = bond_shift.transpose(0, 1, 3, 2)
-    small = [x_back(), y_back(), turn_columns(), same_frequency()]
-    small = [jnp.asarray(table) for table in small]
-    large = [
-        crossed, jnp.asarray(spread_source()), jnp.asarray(merge_x()), vertex, bubble,
-        jnp.asarray(y_forward()), jnp.asarray(rolled_rows()), jnp.asarray(split_x()), jnp.asarray(gather_rows()),
+    operands = [
+        crossed, spread_source(), merge_x(), pair_map, bond_shift, envelope, vertex, bubble, same_frequency(),
+        turn_columns(), y_forward(), rolled_rows(), x_back(), y_back(), split_x(), gather_rows(),
     ]
-    smem = pl.BlockSpec(memory_space=pltpu.SMEM)
-    vmem = pl.BlockSpec(memory_space=pltpu.VMEM)
+    operands = [jnp.asarray(operand) for operand in operands]
     hbm = pl.BlockSpec(memory_space=pl.ANY)
-    return pl.pallas_call(
+    result = pl.pallas_call(
         main_kernel,
         out_shape=jax.ShapeDtypeStruct(vertex.shape, bf16),
-        in_specs=[smem, smem, vmem] + [vmem] * len(small) + [hbm] * len(large),
-        out_specs=vmem,
-        scratch_shapes=[pltpu.VMEM(array.shape, array.dtype) for array in large] + [
+        in_specs=[hbm] * len(operands),
+        out_specs=pl.BlockSpec(memory_space=pltpu.VMEM),
+        scratch_shapes=[
+            (pltpu.SMEM if array.dtype == jnp.int32 else pltpu.VMEM)(array.shape, array.dtype)
+            for array in operands
+        ] + [
             pltpu.VMEM((4, QX, 20 * NFREQ, 128), f32),
             pltpu.VMEM((DEVICES, SEND_ROWS, 128), bf16),
             pltpu.VMEM((DEVICES, SEND_ROWS, 128), bf16),
@@ -367,7 +367,7 @@
             pltpu.VMEM((QX, 192, 512), bf16),
             pltpu.VMEM((5, 192 * QX, 128), f32),
             pltpu.VMEM((80 * ORDER, 128), f32),
-            pltpu.SemaphoreType.DMA((len(large),)),
+            pltpu.SemaphoreType.DMA((len(operands),)),
             pltpu.SemaphoreType.DMA,
             pltpu.SemaphoreType.DMA((NX,)),
             pltpu.SemaphoreType.DMA,
@@ -376,7 +376,8 @@
         compiler_params=pltpu.CompilerParams(
             collective_id=0, has_side_effects=True, vmem_limit_bytes=60 * 2**20
         ),
-    )(pair_map, bond_shift, envelope, *small, *large)
+    )(*operands)
+    return result
 
 
 def solution(mesh):

time: 55.7 us -> 52.2 us (0.937)
  Pallas kernels: 53.3 us -> 49.8 us
    pallas_call x1, Pallas kernels: 53.3 us -> 49.8 us  [local(): pl.pallas_call(main_kernel, out_shape=jax.ShapeDtypeStruct(vertex.shape,...]
where the time goes in v3:
time: 52.2 us; the launch traced here: 52.1 us
  Pallas kernels  49.8 us (95%)
  local copies, waits for them, and re-layouts  2.24 us (4%)
    pallas_call x1, Pallas kernels, local(): pl.pallas_call(main_kernel, out_shape=jax.ShapeDtypeStruct(vertex.shape,...  49.8 us
    unnamed x1, local copies, waits for them, and re-layouts  2.24 us

profile of v3, /device:TPU:1, one launch (start us, length us, event | category | flops | bytes accessed | tf_op | source)
XLA Modules:
  0.0 52.1 jit_solution(15637415040574397557)
XLA Ops:
  0.0 49.8 %shard_map.154 = bf16[5,10,6400]{2,1,0:T(8,128)(2,1)} custom-call(bf16[50,2,6400]{2,1,0:T(2,128)(2,1)} %bitcast.7, bf16[624,512]{1,0:T(8,128)(2,1)} %constant.20.clone.refs_1_, bf16[640,512]{1,0:T(8,128)(2,1)} %constant.21.clone.refs_2_, s32[2,25]{1,0:T(2,128)} %refs_3_.1, s32[2,5,2,5]{3,2,1,0:T(2,128)} %bitcast.9, f32[2,80,80]{2,1,0:T(8,128)} %refs_5_.1, ...), custom_call_target="tpu_custom_call" | custom-call | tf_op jit(solution)/shard_map/pallas_call | solution.py:345
  49.8 2.2 %copy.18 = bf16[5,10,6400]{2,1,0:T(8,128)(2,1)} copy(bf16[5,10,6400]{2,1,0:T(8,128)(2,1)} %shard_map.154) | data formatting | bytes 1280000

commit v4 on v3

--- a/solution.py
+++ b/solution.py
@@ -106,9 +106,10 @@
 
 def partner_order():
     offsets = [(z, y, x, c) for z in range(4) for y in range(4) for x in range(4) for c in range(2)]
+    offsets = [offset for offset in offsets if offset != (0, 0, 0, 0)]
+    draw = np.random.RandomState(1).permutation(len(offsets))
     links = [sum(min(step, 4 - step) for step in offset[:3]) for offset in offsets]
-    ranked = sorted(zip(links, offsets), key=lambda pair: -pair[0])
-    return [offset for _, offset in ranked if offset != (0, 0, 0, 0)]
+    return [offsets[k] for k in sorted(range(len(offsets)), key=lambda k: (-links[k], draw[k]))]
 
 
 def partners(mx, my):

time: 52.2 us -> 51.6 us (0.989)
  Pallas kernels: 49.8 us -> 49.2 us
    pallas_call x1, Pallas kernels: 49.8 us -> 49.2 us  [local(): pl.pallas_call(main_kernel, out_shape=jax.ShapeDtypeStruct(vertex.shape,...]
where the time goes in v4:
time: 51.6 us; the launch traced here: 51.4 us
  Pallas kernels  49.2 us (95%)
  local copies, waits for them, and re-layouts  2.24 us (4%)
    pallas_call x1, Pallas kernels, local(): pl.pallas_call(main_kernel, out_shape=jax.ShapeDtypeStruct(vertex.shape,...  49.2 us
    unnamed x1, local copies, waits for them, and re-layouts  2.24 us

profile of v4, /device:TPU:1, one launch (start us, length us, event | category | flops | bytes accessed | tf_op | source)
XLA Modules:
  0.0 51.4 jit_solution(4615701526198659373)
XLA Ops:
  0.0 49.2 %shard_map.154 = bf16[5,10,6400]{2,1,0:T(8,128)(2,1)} custom-call(bf16[50,2,6400]{2,1,0:T(2,128)(2,1)} %bitcast.7, bf16[624,512]{1,0:T(8,128)(2,1)} %constant.20.clone.refs_1_, bf16[640,512]{1,0:T(8,128)(2,1)} %constant.21.clone.refs_2_, s32[2,25]{1,0:T(2,128)} %refs_3_.1, s32[2,5,2,5]{3,2,1,0:T(2,128)} %bitcast.9, f32[2,80,80]{2,1,0:T(8,128)} %refs_5_.1, ...), custom_call_target="tpu_custom_call" | custom-call | tf_op jit(solution)/shard_map/pallas_call | solution.py:346
  49.2 2.2 %copy.18 = bf16[5,10,6400]{2,1,0:T(8,128)(2,1)} copy(bf16[5,10,6400]{2,1,0:T(8,128)(2,1)} %shard_map.154) | data formatting | bytes 1280000

commit v5 on v4

--- a/solution.py
+++ b/solution.py
@@ -355,7 +355,7 @@
             pltpu.VMEM((4, QX, 20 * NFREQ, 128), f32),
             pltpu.VMEM((DEVICES, SEND_ROWS, 128), bf16),
             pltpu.VMEM((DEVICES, SEND_ROWS, 128), bf16),
-            pltpu.VMEM((4, 25 * LAT, 128), f32),
+            pltpu.VMEM((4, 25 * LAT + 32, 128), f32),
             pltpu.VMEM((2, 25 * NX * 8, 128), f32),
             pltpu.VMEM((DEVICES, BACK_ROWS, 128), bf16),
             pltpu.VMEM((DEVICES, BACK_ROWS, 128), bf16),

time: 51.6 us -> 51.5 us (level)
  no operation moved by 1% of the time
where the time goes in v5:
time: 51.5 us; the launch traced here: 51.4 us
  Pallas kernels  49.1 us (95%)
  local copies, waits for them, and re-layouts  2.24 us (4%)
    pallas_call x1, Pallas kernels, local(): pl.pallas_call(main_kernel, out_shape=jax.ShapeDtypeStruct(vertex.shape,...  49.1 us
    unnamed x1, local copies, waits for them, and re-layouts  2.24 us

profile of v5, /device:TPU:1, one launch (start us, length us, event | category | flops | bytes accessed | tf_op | source)
XLA Modules:
  0.0 51.4 jit_solution(6322382425374528512)
XLA Ops:
  0.0 49.1 %shard_map.154 = bf16[5,10,6400]{2,1,0:T(8,128)(2,1)} custom-call(bf16[50,2,6400]{2,1,0:T(2,128)(2,1)} %bitcast.7, bf16[624,512]{1,0:T(8,128)(2,1)} %constant.20.clone.refs_1_, bf16[640,512]{1,0:T(8,128)(2,1)} %constant.21.clone.refs_2_, s32[2,25]{1,0:T(2,128)} %refs_3_.1, s32[2,5,2,5]{3,2,1,0:T(2,128)} %bitcast.9, f32[2,80,80]{2,1,0:T(8,128)} %refs_5_.1, ...), custom_call_target="tpu_custom_call" | custom-call | tf_op jit(solution)/shard_map/pallas_call | solution.py:346
  49.2 2.2 %copy.18 = bf16[5,10,6400]{2,1,0:T(8,128)(2,1)} copy(bf16[5,10,6400]{2,1,0:T(8,128)(2,1)} %shard_map.154) | data formatting | bytes 1280000
